TPU v7x, 32 devices: a whole 2x2x4 slice. The times are simulated.
32 devices in a mesh: row: 8 (over z, x), col: 4 (over y, core).
Axes of the slice: x: 2, y: 2, z: 4, core: 2. Of those that a mesh axis runs over, the one named last changes fastest.
Arguments:
- hidden: bfloat16 [2560, 8192], P('row', 'col'), may hold values from -6 to 6
- w_query: bfloat16 [8192, 8192], P('col', 'row'), may hold values from -0.0625 to 0.0625
- w_keyval: bfloat16 [8192, 2048], P('col', 'row'), may hold values from -0.15625 to 0.15625
- prefix_cache: bfloat16 [2, 16384, 2048], P(None, 'col', 'row'), may hold values from -60 to 60, as said below
- suffix_lengths: int32 [16], replicated, may hold values from 32 to 160, as said below
- group_ids: int32 [16], replicated, may hold values from 0 to 1, as said below
Outputs:
- attended: bfloat16 [2560, 8192], P('col', 'row')
Inputs may be any that keep to these rules, and one draw needn't show every extreme that they name: `suffix_lengths`: every suffix has 32 to 160 live tokens; some request has exactly 160 and some exactly 32. `group_ids`: exactly 8 requests read each prefix. `prefix_cache`: finite values.
All inputs are finite; a program needn't handle non-finite values.
Results may differ from a plain program's by a relative error of at most 0.011.
Values may be sent and summed in bfloat16 or wider, within the bound.
A program may use at most 128 MiB of HBM per device.

v0:
```python
import jax
import jax.numpy as jnp
from jax import lax
from jax.sharding import PartitionSpec as P

HD = 128
PREFIX = 16384
SUF = 160


def partner(value, axis, stride):
    mask = 2**stride
    pairs = [(source, source ^ mask) for source in range(lax.axis_size(axis))]
    return lax.ppermute(value, axis, pairs)


def rotary_tables(positions):
    freqs = 500000.0 ** (-(jnp.arange(HD // 2, dtype=jnp.float32) * 2.0 / HD))
    angles = positions.astype(jnp.float32)[:, None] * freqs[None, :]
    return (jnp.cos(angles), jnp.sin(angles))


def rotate(values, cosine, sine):
    first = values[..., : HD // 2]
    second = values[..., HD // 2 :]
    cosine = cosine[:, None, :]
    sine = sine[:, None, :]
    return jnp.concatenate(
        [first * cosine - second * sine, second * cosine + first * sine], axis=-1
    )


def block_size(count):
    size = count
    for _ in range(24):
        if size > 2048 and size % 2 == 0:
            size = size // 2
    return size


def block_stats(req_query, keys, values, scale):
    scores = jnp.einsum("thd,kd->htk", req_query, keys, preferred_element_type=jnp.float32) * scale
    top = jnp.max(scores, axis=-1)
    weights = jnp.exp(scores - top[..., None])
    total = jnp.sum(weights, axis=-1)
    accum = jnp.einsum(
        "htk,kd->htd", weights.astype(jnp.bfloat16), values, preferred_element_type=jnp.float32
    )
    return (top, total, accum)


def combine(first, second):
    top = jnp.maximum(first[0], second[0])
    scale_one = jnp.exp(first[0] - top)
    scale_two = jnp.exp(second[0] - top)
    total = first[1] * scale_one + second[1] * scale_two
    accum = first[2] * scale_one[..., None] + second[2] * scale_two[..., None]
    return (top, total, accum)


def empty_state(heads_here):
    return (
        jnp.full((heads_here, SUF), -1e30, jnp.float32),
        jnp.zeros((heads_here, SUF), jnp.float32),
        jnp.zeros((heads_here, SUF, HD), jnp.float32),
    )


def attend_keys(req_query, keys, values, scale):
    count = keys.shape[0]
    size = block_size(count)
    key_blocks = keys.reshape(count // size, size, HD)
    value_blocks = values.reshape(count // size, size, HD)

    def advance(state, pieces):
        return (combine(state, block_stats(req_query, pieces[0], pieces[1], scale)), None)

    state, _ = lax.scan(advance, empty_state(req_query.shape[1]), (key_blocks, value_blocks))
    return state


def per_device(hidden, w_query, w_keyval, prefix_cache, suffix_lengths, group_ids):
    n_col = lax.axis_size("col")
    row_id = lax.axis_index("row")
    col_id = lax.axis_index("col")
    heads_here = w_query.shape[1] // HD
    segments = w_keyval.shape[1] // HD
    scale = 1.0 / HD**0.5
    gathered = lax.all_gather(hidden, "row", axis=0, tiled=True)
    weights_all = jnp.concatenate([w_query, w_keyval], axis=1)
    tok_block = gathered.shape[0] // n_col
    projected = lax.psum_scatter(
        jnp.dot(gathered, weights_all, preferred_element_type=jnp.float32),
        "col",
        scatter_dimension=0,
        tiled=True,
    )
    req_here = tok_block // SUF
    positions = PREFIX + jnp.arange(tok_block, dtype=jnp.int32) % SUF
    cosine, sine = rotary_tables(positions)
    query = projected[:, : heads_here * HD].reshape(tok_block, heads_here, HD)
    query = rotate(query, cosine, sine).astype(jnp.bfloat16)
    keyval = projected[:, heads_here * HD :].reshape(tok_block, segments, HD)
    segment_ids = row_id * segments + jnp.arange(segments, dtype=jnp.int32)
    is_key = segment_ids % 2 == 0
    keyval = jnp.where(is_key[None, :, None], rotate(keyval, cosine, sine), keyval).astype(
        jnp.bfloat16
    )
    cache = prefix_cache.reshape(prefix_cache.shape[0], prefix_cache.shape[1], segments, HD)
    if segments == 1:
        other_keyval, other_cache = partner((keyval, cache), "row", 0)
        is_even = row_id % 2 == 0
        suffix_keys = jnp.where(is_even, keyval[:, 0], other_keyval[:, 0])
        suffix_values = jnp.where(is_even, other_keyval[:, 0], keyval[:, 0])
        cache_keys = jnp.where(is_even, cache[:, :, 0], other_cache[:, :, 0])
        cache_values = jnp.where(is_even, other_cache[:, :, 0], cache[:, :, 0])
    else:
        suffix_keys = keyval[:, 0]
        suffix_values = keyval[:, 1]
        cache_keys = cache[:, :, 0]
        cache_values = cache[:, :, 1]
    req_query = query.reshape(req_here, SUF, heads_here, HD)
    first_req = col_id * req_here
    lengths_here = lax.dynamic_slice_in_dim(suffix_lengths, first_req, req_here)
    groups_here = lax.dynamic_slice_in_dim(group_ids, first_req, req_here)
    start_state = jax.tree.map(
        lambda leaf: jnp.broadcast_to(leaf, (req_here,) + leaf.shape), empty_state(heads_here)
    )
    piece_keys = lax.all_gather(cache_keys, "col", axis=1, tiled=True)
    piece_values = lax.all_gather(cache_values, "col", axis=1, tiled=True)

    def per_request(inputs_one):
        one_query, group, top, total, accum = inputs_one
        keys = lax.dynamic_index_in_dim(piece_keys, group, 0, keepdims=False)
        values = lax.dynamic_index_in_dim(piece_values, group, 0, keepdims=False)
        return combine((top, total, accum), attend_keys(one_query, keys, values, scale))

    prefix_state = lax.map(
        per_request, (req_query, groups_here, start_state[0], start_state[1], start_state[2])
    )
    own_keys = suffix_keys.reshape(req_here, SUF, HD)
    own_values = suffix_values.reshape(req_here, SUF, HD)

    def finish(inputs_one):
        one_query, keys, values, length, top, total, accum = inputs_one
        places = jnp.arange(SUF, dtype=jnp.int32)
        mask = (places[None, :] <= places[:, None]) & (places[None, :] < length)
        scores = (
            jnp.einsum("thd,kd->htk", one_query, keys, preferred_element_type=jnp.float32) * scale
        )
        scores = jnp.where(mask[None], scores, -1e30)
        own_top = jnp.max(scores, axis=-1)
        weights = jnp.exp(scores - own_top[..., None])
        own_total = jnp.sum(weights, axis=-1)
        own_accum = jnp.einsum(
            "htk,kd->htd", weights.astype(jnp.bfloat16), values, preferred_element_type=jnp.float32
        )
        merged = combine((top, total, accum), (own_top, own_total, own_accum))
        result = merged[2] / merged[1][..., None]
        live = (places < length).astype(jnp.float32)
        result = result * live[None, :, None]
        return jnp.transpose(result, (1, 0, 2))

    output = lax.map(
        finish,
        (
            req_query,
            own_keys,
            own_values,
            lengths_here,
            prefix_state[0],
            prefix_state[1],
            prefix_state[2],
        ),
    )
    return output.reshape(tok_block, heads_here * HD).astype(jnp.bfloat16)


def solution(mesh):
    return jax.shard_map(
        per_device,
        mesh=mesh,
        in_specs=(
            P("row", "col"),
            P("col", "row"),
            P("col", "row"),
            P(None, "col", "row"),
            P(),
            P(),
        ),
        out_specs=P("col", "row"),
        check_vma=False,
    )
```

profile of v0, /device:TPU:0, one launch (start us, length us, event | category | flops | bytes accessed | tf_op | source)
XLA Modules:
  0.0 779.5 jit_solution(11184093057173334002)
XLA Ops:
  7.3 155.8 %all-gather.6.cloned.1.call-done = bf16[2560,2048]{1,0:T(8,128)(2,1)} async-done(((bf16[320,2048]{1,0:T(8,128)(2,1)}), bf16[2560,2048]{1,0:T(8,128)(2,1)}) %all-gather.6.cloned.1.call-update) | async-done | bytes 10485776 | tf_op jit(solution)/shard_map/all_gather | solution.py:89
  163.1 21.0 %convolution_bitcast_fusion = f32[2560,1280]{0,1:T(8,128)} fusion(bf16[2560,2048]{1,0:T(8,128)(2,1)} %all-gather.6.cloned.1.call-done, bf16[2048,256]{1,0:T(8,128)(2,1)} %param.14, bf16[2048,1024]{1,0:T(8,128)(2,1)} %param.13), kind=kOutput, calls=%fused_computation.66 | convolution fusion | flops 13432258560 | bytes 28835840 | tf_op jit(solution)/shard_map/dot_general | solution.py:93
  184.2 6.5 copy.12
  190.7 6.4 fusion.63
  199.1 85.8 %reduce-scatter.2.cloned.1.call-done = f32[640,1280]{0,1:T(8,128)} async-done(((f32[2560,1280]{0,1:T(8,128)}), f32[640,1280]{0,1:T(8,128)}) %reduce-scatter.2.cloned.1.call-update) | async-done | bytes 3276816 | tf_op jit(solution)/shard_map/reduce_scatter | solution.py:92
  294.4 3.2 copy.15
  297.6 47.3 %all-gather.10.cloned.1.call-done = bf16[2,16384,1,128]{1,3,2,0:T(8,128)(2,1)} async-done(((bf16[2,4096,1,128]{1,3,2,0:T(8,128)(2,1)}), bf16[2,16384,1,128]{1,3,2,0:T(8,128)(2,1)}) %all-gather.10.cloned.1.call-update) | async-done | bytes 8388624 | tf_op jit(solution)/shard_map/all_gather | solution.py:130
  344.9 59.7 %all-gather.8.cloned.1.call-done = bf16[2,16384,1,128]{1,3,2,0:T(8,128)(2,1)} async-done(((bf16[2,4096,1,128]{1,3,2,0:T(8,128)(2,1)}), bf16[2,16384,1,128]{1,3,2,0:T(8,128)(2,1)}) %all-gather.8.cloned.1.call-update) | async-done | bytes 8388624 | tf_op jit(solution)/shard_map/all_gather | solution.py:129
  404.6 340.6 %while.40 = (s32[]{:T(128)}, f32[4,8,160]{2,1,0:T(8,128)S(1)}, f32[4,8,160]{2,1,0:T(8,128)S(1)}, f32[4,8,160,128]{3,2,1,0:T(8,128)}, s32[4]{0:T(128)S(1)}, /*ind...) while((s32[]{:T(128)}, f32[4,8,160]{2,1,0:T(8,128)S(1)}, ...), condition=%wide.region_6.7_spmd, body=%wide.region_1.6_spmd.sunk | while | flops 1364152320 | bytes 69795200 | solution.py:138
  407.1 7.6 constant_dynamic-slice_fusion.3
  414.7 6.4 copy.28
  421.1 6.4 copy.29
  427.5 60.9 %while.42 = (s32[]{:T(128)}, f32[8,160]{1,0:T(8,128)S(1)}, f32[8,160]{1,0:T(8,128)S(1)}, f32[8,160,128]{2,1,0:T(8,128)S(1)}, bf16[8,2048,128]{2,1,0:T(8,128)(2,1...) while((s32[]{:T(128)}, f32[8,160]{1,0:T(8,128)S(1)}, ...), condition=%wide.region_5.5_spmd.clone, body=%wide.region_2.4_spmd.clone.sunk | while | flops 1363811840 | bytes 34216052 | solution.py:78
  432.1 3.0 fusion.94
  447.3 3.0 fusion.94
  454.9 3.0 fusion.94
  462.5 3.0 fusion.94
  470.2 3.0 fusion.94
  477.8 3.0 fusion.94
  485.4 3.0 fusion.94
  492.3 7.6 constant_dynamic-slice_fusion.3
  499.9 6.4 copy.28
  506.2 6.4 copy.29
  512.7 60.9 %while.42 = (s32[]{:T(128)}, f32[8,160]{1,0:T(8,128)S(1)}, f32[8,160]{1,0:T(8,128)S(1)}, f32[8,160,128]{2,1,0:T(8,128)S(1)}, bf16[8,2048,128]{2,1,0:T(8,128)(2,1...) while((s32[]{:T(128)}, f32[8,160]{1,0:T(8,128)S(1)}, ...), condition=%wide.region_5.5_spmd.clone, body=%wide.region_2.4_spmd.clone.sunk | while | flops 1363811840 | bytes 34216052 | solution.py:78
  517.2 3.0 fusion.94
  524.8 3.0 fusion.94
  532.5 3.0 fusion.94
  540.1 3.0 fusion.94
  547.7 3.0 fusion.94
  555.3 3.0 fusion.94
  563.0 3.0 fusion.94
  570.6 3.0 fusion.94
  577.5 7.6 constant_dynamic-slice_fusion.3
  585.1 6.4 copy.28
  591.4 6.4 copy.29
  597.8 60.9 %while.42 = (s32[]{:T(128)}, f32[8,160]{1,0:T(8,128)S(1)}, f32[8,160]{1,0:T(8,128)S(1)}, f32[8,160,128]{2,1,0:T(8,128)S(1)}, bf16[8,2048,128]{2,1,0:T(8,128)(2,1...) while((s32[]{:T(128)}, f32[8,160]{1,0:T(8,128)S(1)}, ...), condition=%wide.region_5.5_spmd.clone, body=%wide.region_2.4_spmd.clone.sunk | while | flops 1363811840 | bytes 34216052 | solution.py:78
  617.6 3.0 fusion.94
  640.5 3.0 fusion.94
  655.8 3.0 fusion.94
  662.6 7.6 constant_dynamic-slice_fusion.3
  670.2 6.4 copy.28
  676.6 6.4 copy.29
  683.0 60.9 %while.42 = (s32[]{:T(128)}, f32[8,160]{1,0:T(8,128)S(1)}, f32[8,160]{1,0:T(8,128)S(1)}, f32[8,160,128]{2,1,0:T(8,128)S(1)}, bf16[8,2048,128]{2,1,0:T(8,128)(2,1...) while((s32[]{:T(128)}, f32[8,160]{1,0:T(8,128)S(1)}, ...), condition=%wide.region_5.5_spmd.clone, body=%wide.region_2.4_spmd.clone.sunk | while | flops 1363811840 | bytes 34216052 | solution.py:78
  687.6 3.0 fusion.94
  702.8 3.0 fusion.94
  710.4 3.0 fusion.94
  725.7 3.0 fusion.94
  745.3 24.4 %while.41 = (s32[]{:T(128)}, bf16[4,160,8,128]{3,1,2,0:T(8,128)(2,1)}, f32[4,8,160,128]{3,2,1,0:T(8,128)}, f32[4,8,160]{2,1,0:T(8,128)S(1)}, s32[4]{0:T(128)S(1)...) while((s32[]{:T(128)}, ...), condition=%wide.region_10.11_spmd, body=%wide.region_7.10_spmd.sunk | while | flops 107167040 | bytes 15309945 | solution.py:164
  (220 shorter events, 223.7 us)
Async XLA Ops:
  6.5 156.6 %all-gather.6.cloned.1.call-start = ((), (), s32[]{:S(2)}) async-start(), calls=%async_computation.1 | async-start | bytes 11796480 | tf_op jit(solution)/shard_map/all_gather | solution.py:89
  7.3 277.7 %reduce-scatter.2.cloned.1.call-start = ((), (), s32[]{:S(2)}) async-start(), calls=%async_computation.2 | async-start | bytes 16384000 | tf_op jit(solution)/shard_map/reduce_scatter | solution.py:92
  184.1 160.7 %all-gather.10.cloned.1.call-start = ((), (), s32[]{:S(2)}) async-start(), calls=%async_computation.4 | async-start | bytes 10485760 | tf_op jit(solution)/shard_map/all_gather | solution.py:130
  197.1 0.7 copy-start.2
  197.1 1.2 copy-start.3
  197.1 207.5 %all-gather.8.cloned.1.call-start = ((), (), s32[]{:S(2)}) async-start(), calls=%async_computation.3 | async-start | bytes 10485760 | tf_op jit(solution)/shard_map/all_gather | solution.py:129
  288.0 1.7 slice-start
  404.6 340.7 %copy-start.4 = (s32[4]{0:T(128)S(1)}, s32[4]{0:T(128)}, u32[]{:S(2)}) copy-start(s32[4]{0:T(128)} %dynamic_slice.56) | copy-start | bytes 52
  745.3 2.9 copy-start
  750.3 1.1 copy-start.1
  751.4 2.9 copy-start
  756.4 1.1 copy-start.1
  757.5 2.9 copy-start
  762.5 1.1 copy-start.1
  763.6 2.9 copy-start
  768.6 1.1 copy-start.1
Sparse Core Ops, SparseCore 0:
  9.5 153.5 all-gather.5
  184.2 100.6 reduce-scatter.1
  286.5 58.2 all-gather.9
  346.3 58.2 all-gather.7
where the time goes:
time: 784 us; the launch traced here: 779 us
  waiting for transfers between devices  350 us (45%)
  matrix products  216 us (28%)
  local copies, waits for them, and re-layouts  117 us (15%)
  other arithmetic  74.2 us (9%)
  between operations  13.3 us (2%)
  loops' own time  8.75 us (1%)
    all_gather x1, waiting for transfers between devices, per_device(): gathered = lax.all_gather(hidden, 'row', axis=0, tiled=True)  156 us
    dot_general x32, matrix products, block_stats(): jnp.einsum('htk,kd->htd', weights.astype(jnp.bfloat16), values, preferred...  96.6 us
    reduce_scatter x1, waiting for transfers between devices, per_device(): lax.psum_scatter(jnp.dot(gathered, weights_all, preferred_element_type=jn...  85.8 us
    dot_general x32, matrix products, block_stats(): jnp.einsum('thd,kd->htk', req_query, keys, preferred_element_type=jnp.flo...  85.5 us
    reduce_sum x32, other arithmetic, block_stats(): total = jnp.sum(weights, axis=-1)  60.2 us
    all_gather x1, waiting for transfers between devices, per_device(): piece_keys = lax.all_gather(cache_keys, 'col', axis=1, tiled=True)  59.7 us
    dynamic_slice x8, local copies, waits for them, and re-layouts, per_request(): values = lax.dynamic_index_in_dim(piece_values, group, 0, keepdims=False)  56.1 us
    all_gather x1, waiting for transfers between devices, per_device(): piece_values = lax.all_gather(cache_values, 'col', axis=1, tiled=True)  47.3 us
  transfers between devices with their start and end apart: 4, of which 4 were waited for; matrix products, arithmetic and copies ran while one was open for 3% of the time, Pallas kernels for 0%

commit v1 on v0

v1 whole, which is shorter than its diff:
```python
import functools
import math

import jax
import jax.numpy as jnp
from jax import lax
from jax.experimental import pallas as pl
from jax.experimental.pallas import tpu as pltpu
from jax.sharding import PartitionSpec as P

HD = 128
PREFIX = 16384
SUF = 160
SUF_PAD = 256
MASKED = -1e30


def swap(value, axis, mask):
    pairs = [(source, source ^ mask) for source in range(lax.axis_size(axis))]
    return lax.ppermute(value, axis, pairs)


def shift(value, axis, step):
    size = lax.axis_size(axis)
    return lax.ppermute(value, axis, [(source, (source + step) % size) for source in range(size)])


def rotary_tables(positions):
    freqs = 500000.0 ** (-(jnp.arange(HD // 2, dtype=jnp.float32) * 2.0 / HD))
    angles = positions.astype(jnp.float32)[:, None] * freqs[None, :]
    return (jnp.cos(angles), jnp.sin(angles))


def rotate(values, cosine, sine):
    first = values[..., : HD // 2]
    second = values[..., HD // 2 :]
    cosine = cosine[:, None, :]
    sine = sine[:, None, :]
    return jnp.concatenate(
        [first * cosine - second * sine, second * cosine + first * sine], axis=-1
    )


def scores_of(query, keys):
    return lax.dot_general(
        query, keys, (((1,), (1,)), ((), ())), preferred_element_type=jnp.float32
    )


def attend_kernel(n_pieces, tile, pair, groups, lengths, q_ref, own_ref, *refs):
    pieces = refs[:n_pieces]
    out_ref, accum_ref, top_ref, values_ref = refs[n_pieces:]
    request, block, n_blocks = pl.program_id(0), pl.program_id(1), pl.num_programs(1)
    length = lengths[request]
    block_keys = pieces[0].shape[1]
    rows = pair * SUF
    n_pairs = q_ref.shape[1] // (pair * HD)

    @pl.when((request == 0) & (block == 0))
    def _():
        values_ref[:, :, HD:] = jnp.ones((n_pieces, block_keys, HD), jnp.bfloat16)

    for place in range(n_pieces):
        values_ref[place, :, :HD] = pieces[place][0, :, HD:]

    def places(columns):
        row = lax.broadcasted_iota(jnp.int32, (SUF, columns), 0)
        return jnp.concatenate([row] * pair, axis=0)

    def per_pair(index, carry):
        here = pl.ds(pl.multiple_of(index * rows, 32), rows)
        query = jnp.concatenate(
            [
                q_ref[:, pl.ds(pl.multiple_of((index * pair + head) * HD, HD), HD)]
                for head in range(pair)
            ],
            axis=0,
        )

        @pl.when(block == 0)
        def _():
            scores = scores_of(query, own_ref[:, :HD])
            column = lax.broadcasted_iota(jnp.int32, (rows, SUF_PAD), 1)
            mask = (column <= places(SUF_PAD)) & (column < length)
            scores = jnp.where(mask, scores, MASKED)
            top = jnp.max(scores, axis=1, keepdims=True)
            weights = jnp.where(mask, jnp.exp2(scores - top), 0.0).astype(jnp.bfloat16)
            own_values = jnp.concatenate(
                [own_ref[:, HD:], jnp.ones((SUF_PAD, HD), jnp.bfloat16)], axis=1
            )
            accum_ref[here, :] = jnp.dot(weights, own_values, preferred_element_type=jnp.float32)
            top_ref[here, :] = jnp.broadcast_to(top, (rows, HD))

        accum = accum_ref[here, :]
        top = top_ref[here, :1]
        spots = [(place, at) for place in range(n_pieces) for at in range(0, block_keys, tile)]

        def score_tile(spot):
            return scores_of(query, pieces[spot[0]][0, spot[1] : spot[1] + tile, :HD])

        ahead = score_tile(spots[0])
        for number, (place, at) in enumerate(spots):
            scores = ahead
            if number + 1 < len(spots):
                ahead = score_tile(spots[number + 1])
            new_top = jnp.maximum(top, jnp.max(scores, axis=1, keepdims=True))
            weights = jnp.exp2(scores - new_top).astype(jnp.bfloat16)
            accum = accum * jnp.exp2(top - new_top) + jnp.dot(
                weights, values_ref[place, at : at + tile, :], preferred_element_type=jnp.float32
            )
            top = new_top
        accum_ref[here, :] = accum
        top_ref[here, :] = jnp.broadcast_to(top, (rows, HD))

        @pl.when(block == n_blocks - 1)
        def _():
            result = accum[:, :HD] / accum[:, HD:]
            result = jnp.where(places(HD) < length, result, 0.0).astype(out_ref.dtype)
            for head in range(pair):
                out_ref[:, pl.ds(pl.multiple_of((index * pair + head) * HD, HD), HD)] = result[
                    head * SUF : (head + 1) * SUF
                ]

        return carry

    lax.fori_loop(0, n_pairs, per_pair, 0)


def attend(query, own, pieces, groups, lengths):
    n_requests = query.shape[0] // SUF
    width = query.shape[1]
    n_pieces = len(pieces)
    block_keys = min(2048, pieces[0].shape[1])
    n_blocks = pieces[0].shape[1] // block_keys
    tile = min(2048, block_keys)
    pair = 2
    heads = width // HD
    keys = PREFIX + SUF
    flops = 4 * n_requests * SUF * heads * keys * HD
    grid_spec = pltpu.PrefetchScalarGridSpec(
        num_scalar_prefetch=2,
        grid=(n_requests, n_blocks),
        in_specs=[
            pl.BlockSpec((SUF, width), lambda i, j, g, n: (i, 0)),
            pl.BlockSpec((SUF_PAD, 2 * HD), lambda i, j, g, n: (i, 0)),
        ]
        + [pl.BlockSpec((1, block_keys, 2 * HD), lambda i, j, g, n: (g[i], j, 0))] * n_pieces,
        out_specs=pl.BlockSpec((SUF, width), lambda i, j, g, n: (i, 0)),
        scratch_shapes=[
            pltpu.VMEM((heads * SUF, 2 * HD), jnp.float32),
            pltpu.VMEM((heads * SUF, HD), jnp.float32),
            pltpu.VMEM((n_pieces, block_keys, 2 * HD), jnp.bfloat16),
        ],
    )
    return pl.pallas_call(
        functools.partial(attend_kernel, n_pieces, tile, pair),
        grid_spec=grid_spec,
        out_shape=jax.ShapeDtypeStruct(query.shape, jnp.bfloat16),
        compiler_params=pltpu.CompilerParams(
            dimension_semantics=("arbitrary", "arbitrary"), vmem_limit_bytes=56 * 2**20
        ),
        cost_estimate=pl.CostEstimate(
            flops=2 * flops,
            bytes_accessed=n_requests * keys * 4 * HD,
            transcendentals=n_requests * SUF * heads * keys,
        ),
        name="attend",
    )(groups, lengths, query, own, *pieces)


def per_device(hidden, w_query, w_keyval, prefix_cache, suffix_lengths, group_ids):
    n_row = lax.axis_size("row")
    n_col = lax.axis_size("col")
    row_id = lax.axis_index("row")
    col_id = lax.axis_index("col")
    heads_here = w_query.shape[1] // HD
    segments = w_keyval.shape[1] // HD
    n_chunks = hidden.shape[0] // SUF
    shards_per_col = n_row // n_col
    col_tokens = shards_per_col * SUF
    col_bits = n_col.bit_length() - 1

    cache = prefix_cache
    if segments == 1:
        other = swap(cache, "row", 1)
        is_even = row_id % 2 == 0
        cache = jnp.concatenate(
            [jnp.where(is_even, cache, other), jnp.where(is_even, other, cache)], axis=-1
        )
    pieces = [cache]
    for bit in reversed(range(col_bits)):
        pieces = pieces + [swap(piece, "col", 2**bit) for piece in pieces]

    weights_all = jnp.concatenate([w_query, w_keyval], axis=1)
    width = weights_all.shape[1]
    positions = PREFIX + jnp.arange(col_tokens, dtype=jnp.int32) % SUF
    cosine, sine = rotary_tables(positions)
    factor = math.log2(math.e) / HD**0.5
    lengths_all = suffix_lengths.reshape(n_col, shards_per_col, n_chunks)
    groups_all = group_ids.reshape(n_col, shards_per_col, n_chunks)
    lengths_here = lax.dynamic_index_in_dim(lengths_all, col_id, 0, keepdims=False)
    groups_here = lax.dynamic_index_in_dim(groups_all, col_id, 0, keepdims=False)

    outputs = []
    for chunk in range(n_chunks):
        block = hidden[chunk * SUF : (chunk + 1) * SUF]
        gathered = jnp.zeros((n_row,) + block.shape, block.dtype)
        for step in range(n_row // 2):
            if step:
                block = shift(block, "row", 2)
            other = swap(block, "row", 1)
            source = (row_id - 2 * step) % n_row
            gathered = lax.dynamic_update_index_in_dim(gathered, block, source, 0)
            gathered = lax.dynamic_update_index_in_dim(gathered, other, source ^ 1, 0)
        partial = jnp.dot(
            gathered.reshape(n_row * SUF, -1), weights_all, preferred_element_type=jnp.float32
        )

        partial = partial.reshape(n_col, col_tokens, width)
        for bit in range(col_bits):
            mine = (col_id // 2**bit) % 2
            halves = partial.reshape(partial.shape[0] // 2, 2, col_tokens, width)
            kept = lax.dynamic_index_in_dim(halves, mine, 1, keepdims=False)
            given = lax.dynamic_index_in_dim(halves, 1 - mine, 1, keepdims=False)
            if bit:
                given = given.astype(jnp.bfloat16)
            partial = kept + swap(given, "col", 2**bit).astype(jnp.float32)
        projected = partial.reshape(col_tokens, width)

        query = projected[:, : heads_here * HD].reshape(col_tokens, heads_here, HD)
        query = (rotate(query, cosine, sine) * factor).astype(jnp.bfloat16)
        query = query.reshape(col_tokens, heads_here * HD)
        keyval = projected[:, heads_here * HD :].reshape(col_tokens, segments, HD)
        segment_ids = row_id * segments + jnp.arange(segments, dtype=jnp.int32)
        is_key = segment_ids % 2 == 0
        keyval = jnp.where(is_key[None, :, None], rotate(keyval, cosine, sine), keyval)
        keyval = keyval.astype(jnp.bfloat16).reshape(col_tokens, segments * HD)
        if segments == 1:
            other = swap(keyval, "row", 1)
            is_even = row_id % 2 == 0
            keyval = jnp.concatenate(
                [jnp.where(is_even, keyval, other), jnp.where(is_even, other, keyval)], axis=-1
            )
        own = keyval.reshape(shards_per_col, SUF, 2 * HD)
        own = jnp.pad(own, ((0, 0), (0, SUF_PAD - SUF), (0, 0)))
        own = own.reshape(shards_per_col * SUF_PAD, 2 * HD)
        outputs.append(
            attend(query, own, pieces, groups_here[:, chunk], lengths_here[:, chunk])
        )
    if n_chunks == 1:
        return outputs[0]
    parts = [one.reshape(shards_per_col, 1, SUF, heads_here * HD) for one in outputs]
    return jnp.concatenate(parts, axis=1).reshape(-1, heads_here * HD)


def solution(mesh):
    return jax.shard_map(
        per_device,
        mesh=mesh,
        in_specs=(
            P("row", "col"),
            P("col", "row"),
            P("col", "row"),
            P(None, "col", "row"),
            P(),
            P(),
        ),
        out_specs=P("col", "row"),
        check_vma=False,
    )
```

time: 784 us -> 341 us (0.43)
  waiting for transfers between devices: 350 us -> 129 us
  matrix products: 216 us -> 16.1 us
  Pallas kernels: 0 us -> 129 us
  local copies, waits for them, and re-layouts: 117 us -> 35.7 us
  other arithmetic: 74.2 us -> 14.5 us
  starting transfers between devices: 0.3 us -> 15.3 us
  between operations: 13.3 us -> 0.35 us
  loops' own time: 8.75 us -> 0 us
    all_gather x3 -> x0, waiting for transfers between devices: 263 us -> none  [the longest x1 156 us: per_device(): gathered = lax.all_gather(hidden, 'row', axis=0, tiled=True)]
    dot_general x73 -> x2, matrix products: 216 us -> 16.1 us  [per_device(): jnp.dot(gathered.reshape(n_row * SUF, -1), weights_all, preferred_element...]
    ppermute x0 -> x21, waiting for transfers between devices: none -> 129 us  [the longest x6 70 us: shift(): lax.ppermute(value, axis, [(source, (source + step) % size) for source in...]
    pallas_call x0 -> x2, Pallas kernels: none -> 129 us  [attend(): pl.pallas_call(functools.partial(attend_kernel, n_pieces, tile, pair), gr...]
    dynamic_slice x22 -> x0, local copies, waits for them, and re-layouts: 87.3 us -> none  [the longest x8 56.1 us: per_request(): values = lax.dynamic_index_in_dim(piece_values, group, 0, keepdims=False)]
    reduce_scatter x1 -> x0, waiting for transfers between devices: 85.8 us -> none  [per_device(): lax.psum_scatter(jnp.dot(gathered, weights_all, preferred_element_type=jn...]
    reduce_sum x36 -> x0, other arithmetic: 61.1 us -> none  [the longest x32 60.2 us: block_stats(): total = jnp.sum(weights, axis=-1)]
    ppermute x0 -> x21, starting transfers between devices: none -> 15.3 us  [the longest x15 12 us: swap(): return lax.ppermute(value, axis, pairs)]
  transfers between devices with their start and end apart: 4 -> 21, of which waited for: 4 -> 10; matrix products, arithmetic and copies ran while one was open for 3% -> 17% of each run, Pallas kernels for 0% -> 0%
where the time goes in v1:
time: 341 us
  waiting for transfers between devices  129 us (38%)
  Pallas kernels  129 us (38%)
  local copies, waits for them, and re-layouts  35.7 us (10%)
  matrix products  16.1 us (5%)
  starting transfers between devices  15.3 us (4%)
  other arithmetic  14.5 us (4%)
    pallas_call x2, Pallas kernels, attend(): pl.pallas_call(functools.partial(attend_kernel, n_pieces, tile, pair), gr...  129 us
    ppermute x6, waiting for transfers between devices, shift(): lax.ppermute(value, axis, [(source, (source + step) % size) for source in...  70 us
    ppermute x15, waiting for transfers between devices, swap(): return lax.ppermute(value, axis, pairs)  59.5 us
    dot_general x2, matrix products, per_device(): jnp.dot(gathered.reshape(n_row * SUF, -1), weights_all, preferred_element...  16.1 us
    ppermute x15, starting transfers between devices, swap(): return lax.ppermute(value, axis, pairs)  12 us
    unnamed x30, local copies, waits for them, and re-layouts  7.22 us
  transfers between devices with their start and end apart: 21, of which 10 were waited for; matrix products, arithmetic and copies ran while one was open for 17% of the time, Pallas kernels for 0%

profile of v1, /device:TPU:0, one launch (start us, length us, event | category | flops | bytes accessed | tf_op | source)
XLA Modules:
  0.0 340.9 jit_solution(14917676256670625271)
XLA Ops:
  0.0 1.5 fusion.15
  1.5 3.0 collective-permute-start
  4.5 1.6 collective-permute-start.1
  6.6 1.6 collective-permute-start.13
  8.2 1.5 collective-permute-start.9
  9.7 3.0 broadcast.125.clone.1
  14.3 9.7 %collective-permute-done.1 = bf16[160,2048]{1,0:T(8,128)(2,1)} collective-permute-done((bf16[160,2048]{1,0:T(8,128)(2,1)S(1)}, bf16[160,2048]{1,0:T(8,128)(2,1)}, u32[]{:S(2)}, u32[]{:S(2)}) %collective-permute-start.1) | collective-permute-done | bytes 655392 | tf_op jit(solution)/shard_map/ppermute | solution.py:25
  24.4 13.6 %collective-permute-done.13 = bf16[160,2048]{1,0:T(8,128)(2,1)S(1)} collective-permute-done((bf16[160,2048]{1,0:T(8,128)(2,1)S(1)}, bf16[160,2048]{1,0:T(8,128)(2,1)S(1)}, u32[]{:S(2)}, u32[]{:S(2)}) %collective-permute-start.13) | collective-permute-done | bytes 655392 | tf_op jit(solution)/shard_map/ppermute | solution.py:25
  38.3 2.0 bitcast_dynamic-update-slice_fusion.14
  40.3 2.0 bitcast_dynamic-update-slice_fusion.13
  42.3 1.1 bitcast_dynamic-update-slice_fusion.6
  43.6 8.5 %collective-permute-done.3 = bf16[160,2048]{1,0:T(8,128)(2,1)S(1)} collective-permute-done((bf16[160,2048]{1,0:T(8,128)(2,1)}, bf16[160,2048]{1,0:T(8,128)(2,1)S(1)}, u32[]{:S(2)}, u32[]{:S(2)}) %collective-permute-start.3) | collective-permute-done | bytes 655392 | tf_op jit(solution)/shard_map/ppermute | solution.py:25
  52.3 13.7 %collective-permute-done.15 = bf16[160,2048]{1,0:T(8,128)(2,1)S(1)} collective-permute-done((bf16[160,2048]{1,0:T(8,128)(2,1)S(1)}, bf16[160,2048]{1,0:T(8,128)(2,1)S(1)}, u32[]{:S(2)}, u32[]{:S(2)}) %collective-permute-start.15) | collective-permute-done | bytes 655392 | tf_op jit(solution)/shard_map/ppermute | solution.py:25
  66.3 0.9 bitcast_dynamic-update-slice_fusion.12
  67.2 0.9 bitcast_dynamic-update-slice_fusion.11
  68.3 24.4 %collective-permute-done.17 = bf16[160,2048]{1,0:T(8,128)(2,1)S(1)} collective-permute-done((bf16[160,2048]{1,0:T(8,128)(2,1)S(1)}, bf16[160,2048]{1,0:T(8,128)(2,1)S(1)}, u32[]{:S(2)}, u32[]{:S(2)}) %collective-permute-start.17) | collective-permute-done | bytes 655392 | tf_op jit(solution)/shard_map/ppermute | solution.py:25
  93.3 1.5 collective-permute-start.6
  94.8 0.9 bitcast_dynamic-update-slice_fusion.10
  95.7 0.9 bitcast_dynamic-update-slice_fusion.9
  96.8 13.6 %collective-permute-done.18 = bf16[160,2048]{1,0:T(8,128)(2,1)S(1)} collective-permute-done((bf16[160,2048]{1,0:T(8,128)(2,1)S(1)}, bf16[160,2048]{1,0:T(8,128)(2,1)S(1)}, u32[]{:S(2)}, u32[]{:S(2)}) %collective-permute-start.18) | collective-permute-done | bytes 655392 | tf_op jit(solution)/shard_map/ppermute | solution.py:20
  110.4 11.7 %collective-permute-done.6 = bf16[160,2048]{1,0:T(8,128)(2,1)S(1)} collective-permute-done((bf16[160,2048]{1,0:T(8,128)(2,1)S(1)}, bf16[160,2048]{1,0:T(8,128)(2,1)S(1)}, u32[]{:S(2)}, u32[]{:S(2)}) %collective-permute-start.6) | collective-permute-done | bytes 655392 | tf_op jit(solution)/shard_map/ppermute | solution.py:20
  122.1 1.0 bitcast_dynamic-update-slice_fusion
  123.2 7.1 %fusion = f32[2,2,320,1280]{3,2,1,0:T(8,128)S(1)} fusion(bf16[2,2,320,2048]{3,2,1,0:T(8,128)(2,1)S(1)} %bitcast.85, bf16[2048,256]{1,0:T(8,128)(2,1)S(1)} %copy-done.9, bf16[2048,1024]{1,0:T(8,128)(2,1)S(1)} %copy-done.8), kind=kOutput, calls=%fused_computation.1 | convolution fusion | flops 6721372160 | bytes 17039360 | tf_op jit(solution)/shard_map/dot_general | solution.py:215
  130.3 2.1 dynamic-slice_bitcast_fusion
  132.4 1.6 copy-done.1
  134.0 9.1 %fusion.1 = f32[2,2,320,1280]{3,2,1,0:T(8,128)S(1)} fusion(bf16[2,2,320,2048]{3,2,1,0:T(8,128)(2,1)} %bitcast.10, bf16[2048,256]{1,0:T(8,128)(2,1)S(1)} %copy-done.9, bf16[2048,1024]{1,0:T(8,128)(2,1)S(1)} %copy-done.8), kind=kOutput, calls=%fused_computation.2 | convolution fusion | flops 6721372160 | bytes 17039360 | tf_op jit(solution)/shard_map/dot_general | solution.py:215
  143.1 2.8 copy-done
  145.8 1.9 dynamic-slice_bitcast_fusion.1
  150.1 3.7 %bitcast_add_fusion = f32[2,320,1280]{2,1,0:T(8,128)S(1)} fusion(f32[2,320,1280]{2,1,0:T(8,128)} %collective-permute-done.19, f32[2,2,320,1280]{3,2,1,0:T(8,128)} %copy-done.1, s32[]{:T(128)S(6)} %select_n.177), kind=kLoop, calls=%fused_computation.3 | loop fusion | flops 819200 | bytes 9830404 | tf_op jit(solution)/shard_map/add | solution.py:227
  153.9 1.6 collective-permute-start.20
  155.5 2.9 collective-permute-done.7
  159.0 1.6 collective-permute-start.8
  160.5 14.6 %collective-permute-done.20 = bf16[1,320,1280]{2,1,0:T(8,128)(2,1)S(1)} collective-permute-done((bf16[1,320,1280]{2,1,0:T(8,128)(2,1)S(1)}, bf16[1,320,1280]{2,1,0:T(8,128)(2,1)S(1)}, u32[]{:S(2)}, u32[]{:S(2)}) %collective-permute-start.20) | collective-permute-done | bytes 819232 | tf_op jit(solution)/shard_map/ppermute | solution.py:20
  175.7 16.7 %collective-permute-done.8 = bf16[1,320,1280]{2,1,0:T(8,128)(2,1)S(1)} collective-permute-done((bf16[1,320,1280]{2,1,0:T(8,128)(2,1)S(1)}, bf16[1,320,1280]{2,1,0:T(8,128)(2,1)S(1)}, u32[]{:S(2)}, u32[]{:S(2)}) %collective-permute-start.8) | collective-permute-done | bytes 819232 | tf_op jit(solution)/shard_map/ppermute | solution.py:20
  193.1 1.1 multiply_subtract_fusion.1
  194.6 1.0 copy.17
  195.6 0.9 reshape.169
  196.5 0.9 reshape.163
  197.4 2.9 multiply_subtract_fusion.3
  200.3 1.1 pad_maximum_fusion.2
  201.4 1.0 concatenate.28
  202.4 2.1 pad_maximum_fusion.1
  204.5 1.7 concatenate.25
  206.7 1.0 copy.16
  209.2 64.7 %attend.2 = bf16[320,1024]{1,0:T(8,128)(2,1)} custom-call(s32[2]{0:T(128)} %get-tuple-element.28.groups, s32[2]{0:T(128)} %get-tuple-element.5.lengths, bf16[320,1024]{1,0:T(8,128)(2,1)} %bitcast.92, bf16[512,256]{1,0:T(8,128)(2,1)} %bitcast.95, bf16[2,4096,256]{2,1,0:T(8,128)(2,1)} %refs_0_.3, bf16[2,4096,256]{2,1,0:T(8,128)(2,1)} %collective-permute-done.9.refs_1_, ...), custom_call_target="tpu_custom_call" | custom-call | flops 43369103360 | bytes 16941056 | tf_op jit(solution)/shard_map/attend/pallas_call | solution.py:155
  273.9 64.6 %attend.3 = bf16[320,1024]{1,0:T(8,128)(2,1)} custom-call(s32[2]{0:T(128)} %get-tuple-element.27.groups, s32[2]{0:T(128)} %get-tuple-element.6.lengths, bf16[320,1024]{1,0:T(8,128)(2,1)} %bitcast.93, bf16[512,256]{1,0:T(8,128)(2,1)} %bitcast.94, bf16[2,4096,256]{2,1,0:T(8,128)(2,1)} %refs_0_.3, bf16[2,4096,256]{2,1,0:T(8,128)(2,1)} %collective-permute-done.9.refs_1_, ...), custom_call_target="tpu_custom_call" | custom-call | flops 43369103360 | bytes 16941056 | tf_op jit(solution)/shard_map/attend/pallas_call | solution.py:155
  338.5 1.2 pad_maximum_fusion
  339.7 1.2 copy.8
  (82 shorter events, 10.9 us)
Async XLA Ops:
  0.0 12.7 %copy-start.2 = (bf16[320,2048]{1,0:T(8,128)(2,1)S(1)}, bf16[320,2048]{1,0:T(8,128)(2,1)}, u32[]{:S(2)}) copy-start(bf16[320,2048]{1,0:T(8,128)(2,1)} %param.6) | copy-start | bytes 3932164
  1.5 22.8 %collective-permute-start = (bf16[160,2048]{1,0:T(8,128)(2,1)S(1)}, bf16[160,2048]{1,0:T(8,128)(2,1)}, u32[]{:S(2)}, u32[]{:S(2)}) collective-permute-start(bf16[160,2048]{1,0:T(8,128)(2,1)S(1)} %get-tuple-element.13), channel_id=1, source_target_pairs={{0,4},{4,0},{8,12},{12,8},{16,20},{20,16},{24,28},{28,24},{1,5},{5... | collective-permute-start | bytes 1966088 | tf_op jit(solution)/shard_map/ppermute | solution.py:20
  4.5 19.6 %collective-permute-start.1 = (bf16[160,2048]{1,0:T(8,128)(2,1)S(1)}, bf16[160,2048]{1,0:T(8,128)(2,1)}, u32[]{:S(2)}, u32[]{:S(2)}) collective-permute-start(bf16[160,2048]{1,0:T(8,128)(2,1)S(1)} %get-tuple-element.13), channel_id=1, source_target_pairs={{0,8},{4,12},{8,16},{12,20},{16,24},{20,28},{24,0},{28,4},{1,9},{5... | collective-permute-start | bytes 1966088 | tf_op jit(solution)/shard_map/ppermute | solution.py:25
  6.1 36.2 %collective-permute-start.12 = (bf16[160,2048]{1,0:T(8,128)(2,1)S(1)}, bf16[160,2048]{1,0:T(8,128)(2,1)}, u32[]{:S(2)}, u32[]{:S(2)}) collective-permute-start(bf16[160,2048]{1,0:T(8,128)(2,1)S(1)} %get-tuple-element.14), channel_id=1, source_target_pairs={{0,4},{4,0},{8,12},{12,8},{16,20},{20,16},{24,28},{28,24},{1,5},{5... | collective-permute-start | bytes 1966088 | tf_op jit(solution)/shard_map/ppermute | solution.py:20
  6.6 31.4 %collective-permute-start.13 = (bf16[160,2048]{1,0:T(8,128)(2,1)S(1)}, bf16[160,2048]{1,0:T(8,128)(2,1)S(1)}, u32[]{:S(2)}, u32[]{:S(2)}) collective-permute-start(bf16[160,2048]{1,0:T(8,128)(2,1)S(1)} %get-tuple-element.14), channel_id=1, source_target_pairs={{0,8},{4,12},{8,16},{12,20},{16,24},{20,28},{24,0},{28,4},{1,9},{5... | collective-permute-start | bytes 1966088 | tf_op jit(solution)/shard_map/ppermute | solution.py:25
  8.2 141.8 %collective-permute-start.9 = (bf16[2,4096,256]{2,1,0:T(8,128)(2,1)}, bf16[2,4096,256]{2,1,0:T(8,128)(2,1)}, u32[]{:S(2)}, u32[]{:S(2)}) collective-permute-start(bf16[2,4096,256]{2,1,0:T(8,128)(2,1)} %refs_0_.3), channel_id=1, source_target_pairs={{0,2},{1,3},{2,0},{3,1},{4,6},{5,7},{6,4},{7,5},{8,10},{9,11},{10,... | collective-permute-start | bytes 12582920 | tf_op jit(solution)/shard_map/ppermute | solution.py:20
  24.0 28.3 %collective-permute-start.2 = (bf16[160,2048]{1,0:T(8,128)(2,1)}, bf16[160,2048]{1,0:T(8,128)(2,1)S(1)}, u32[]{:S(2)}, u32[]{:S(2)}) collective-permute-start(bf16[160,2048]{1,0:T(8,128)(2,1)} %collective-permute-done.1), channel_id=1, source_target_pairs={{0,4},{4,0},{8,12},{12,8},{16,20},{20,16},{24,28},{28,24},{1,5},{5... | collective-permute-start | bytes 1966088 | tf_op jit(solution)/shard_map/ppermute | solution.py:20
  24.3 27.7 %collective-permute-start.3 = (bf16[160,2048]{1,0:T(8,128)(2,1)}, bf16[160,2048]{1,0:T(8,128)(2,1)S(1)}, u32[]{:S(2)}, u32[]{:S(2)}) collective-permute-start(bf16[160,2048]{1,0:T(8,128)(2,1)} %collective-permute-done.1), channel_id=1, source_target_pairs={{0,8},{4,12},{8,16},{12,20},{16,24},{20,28},{24,0},{28,4},{1,9},{5... | collective-permute-start | bytes 1966088 | tf_op jit(solution)/shard_map/ppermute | solution.py:25
  38.0 30.1 %collective-permute-start.14 = (bf16[160,2048]{1,0:T(8,128)(2,1)S(1)}, bf16[160,2048]{1,0:T(8,128)(2,1)S(1)}, u32[]{:S(2)}, u32[]{:S(2)}) collective-permute-start(bf16[160,2048]{1,0:T(8,128)(2,1)S(1)} %collective-permute-done.13), channel_id=1, source_target_pairs={{0,4},{4,0},{8,12},{12,8},{16,20},{20,16},{24,28},{28,24},{1,5},{5... | collective-permute-start | bytes 1966088 | tf_op jit(solution)/shard_map/ppermute | solution.py:20
  42.3 23.8 %collective-permute-start.15 = (bf16[160,2048]{1,0:T(8,128)(2,1)S(1)}, bf16[160,2048]{1,0:T(8,128)(2,1)S(1)}, u32[]{:S(2)}, u32[]{:S(2)}) collective-permute-start(bf16[160,2048]{1,0:T(8,128)(2,1)S(1)} %collective-permute-done.13), channel_id=1, source_target_pairs={{0,8},{4,12},{8,16},{12,20},{16,24},{20,28},{24,0},{28,4},{1,9},{5... | collective-permute-start | bytes 1966088 | tf_op jit(solution)/shard_map/ppermute | solution.py:25
  52.0 42.8 %collective-permute-start.4 = (bf16[160,2048]{1,0:T(8,128)(2,1)S(1)}, bf16[160,2048]{1,0:T(8,128)(2,1)S(1)}, u32[]{:S(2)}, u32[]{:S(2)}) collective-permute-start(bf16[160,2048]{1,0:T(8,128)(2,1)S(1)} %collective-permute-done.3), channel_id=1, source_target_pairs={{0,4},{4,0},{8,12},{12,8},{16,20},{20,16},{24,28},{28,24},{1,5},{5... | collective-permute-start | bytes 1966088 | tf_op jit(solution)/shard_map/ppermute | solution.py:20
  52.3 41.0 %collective-permute-start.5 = (bf16[160,2048]{1,0:T(8,128)(2,1)S(1)}, bf16[160,2048]{1,0:T(8,128)(2,1)S(1)}, u32[]{:S(2)}, u32[]{:S(2)}) collective-permute-start(bf16[160,2048]{1,0:T(8,128)(2,1)S(1)} %collective-permute-done.3), channel_id=1, source_target_pairs={{0,8},{4,12},{8,16},{12,20},{16,24},{20,28},{24,0},{28,4},{1,9},{5... | collective-permute-start | bytes 1966088 | tf_op jit(solution)/shard_map/ppermute | solution.py:25
  66.1 30.6 %collective-permute-start.16 = (bf16[160,2048]{1,0:T(8,128)(2,1)S(1)}, bf16[160,2048]{1,0:T(8,128)(2,1)S(1)}, u32[]{:S(2)}, u32[]{:S(2)}) collective-permute-start(bf16[160,2048]{1,0:T(8,128)(2,1)S(1)} %collective-permute-done.15), channel_id=1, source_target_pairs={{0,4},{4,0},{8,12},{12,8},{16,20},{20,16},{24,28},{28,24},{1,5},{5... | collective-permute-start | bytes 1966088 | tf_op jit(solution)/shard_map/ppermute | solution.py:20
  68.1 24.6 %collective-permute-start.17 = (bf16[160,2048]{1,0:T(8,128)(2,1)S(1)}, bf16[160,2048]{1,0:T(8,128)(2,1)S(1)}, u32[]{:S(2)}, u32[]{:S(2)}) collective-permute-start(bf16[160,2048]{1,0:T(8,128)(2,1)S(1)} %collective-permute-done.15), channel_id=1, source_target_pairs={{0,8},{4,12},{8,16},{12,20},{16,24},{20,28},{24,0},{28,4},{1,9},{5... | collective-permute-start | bytes 1966088 | tf_op jit(solution)/shard_map/ppermute | solution.py:25
  68.3 54.8 %copy-start.8 = (bf16[2048,1024]{1,0:T(8,128)(2,1)S(1)}, bf16[2048,1024]{1,0:T(8,128)(2,1)}, u32[]{:S(2)}) copy-start(bf16[2048,1024]{1,0:T(8,128)(2,1)} %param.7) | copy-start | bytes 12582916
  68.3 54.8 %copy-start.9 = (bf16[2048,256]{1,0:T(8,128)(2,1)S(1)}, bf16[2048,256]{1,0:T(8,128)(2,1)}, u32[]{:S(2)}) copy-start(bf16[2048,256]{1,0:T(8,128)(2,1)} %param.8) | copy-start | bytes 3145732
  92.8 17.7 %collective-permute-start.18 = (bf16[160,2048]{1,0:T(8,128)(2,1)S(1)}, bf16[160,2048]{1,0:T(8,128)(2,1)S(1)}, u32[]{:S(2)}, u32[]{:S(2)}) collective-permute-start(bf16[160,2048]{1,0:T(8,128)(2,1)S(1)} %collective-permute-done.17), channel_id=1, source_target_pairs={{0,4},{4,0},{8,12},{12,8},{16,20},{20,16},{24,28},{28,24},{1,5},{5... | collective-permute-start | bytes 1966088 | tf_op jit(solution)/shard_map/ppermute | solution.py:20
  93.3 28.9 %collective-permute-start.6 = (bf16[160,2048]{1,0:T(8,128)(2,1)S(1)}, bf16[160,2048]{1,0:T(8,128)(2,1)S(1)}, u32[]{:S(2)}, u32[]{:S(2)}) collective-permute-start(bf16[160,2048]{1,0:T(8,128)(2,1)S(1)} %collective-permute-done.5), channel_id=1, source_target_pairs={{0,4},{4,0},{8,12},{12,8},{16,20},{20,16},{24,28},{28,24},{1,5},{5... | collective-permute-start | bytes 1966088 | tf_op jit(solution)/shard_map/ppermute | solution.py:20
  130.3 3.7 %copy-start.1 = (f32[2,2,320,1280]{3,2,1,0:T(8,128)}, f32[2,2,320,1280]{3,2,1,0:T(8,128)S(1)}, u32[]{:S(2)}) copy-start(f32[2,2,320,1280]{3,2,1,0:T(8,128)S(1)} %fusion) | copy-start | bytes 19660804
  132.4 17.7 %collective-permute-start.19 = (f32[2,320,1280]{2,1,0:T(8,128)}, f32[2,320,1280]{2,1,0:T(8,128)}, u32[]{:S(2)}, u32[]{:S(2)}) collective-permute-start(f32[2,320,1280]{2,1,0:T(8,128)} %dynamic-slice_bitcast_fusion), channel_id=1, source_target_pairs={{0,1},{1,0},{2,3},{3,2},{4,5},{5,4},{6,7},{7,6},{8,9},{9,8},{10,11... | collective-permute-start | bytes 9830408 | tf_op jit(solution)/shard_map/ppermute | solution.py:20
  143.1 2.8 copy-start
  145.8 2.4 copy-start.6
  145.8 2.5 copy-start.7
  147.7 10.7 %collective-permute-start.7 = (f32[2,320,1280]{2,1,0:T(8,128)}, f32[2,320,1280]{2,1,0:T(8,128)S(1)}, u32[]{:S(2)}, u32[]{:S(2)}) collective-permute-start(f32[2,320,1280]{2,1,0:T(8,128)} %dynamic-slice_bitcast_fusion.1), channel_id=1, source_target_pairs={{0,1},{1,0},{2,3},{3,2},{4,5},{5,4},{6,7},{7,6},{8,9},{9,8},{10,11... | collective-permute-start | bytes 9830408 | tf_op jit(solution)/shard_map/ppermute | solution.py:20
  147.7 61.5 %collective-permute-start.10 = (bf16[2,4096,256]{2,1,0:T(8,128)(2,1)}, bf16[2,4096,256]{2,1,0:T(8,128)(2,1)}, u32[]{:S(2)}, u32[]{:S(2)}) collective-permute-start(bf16[2,4096,256]{2,1,0:T(8,128)(2,1)} %refs_0_.3), channel_id=1, source_target_pairs={{0,1},{1,0},{2,3},{3,2},{4,5},{5,4},{6,7},{7,6},{8,9},{9,8},{10,11... | collective-permute-start | bytes 12582920 | tf_op jit(solution)/shard_map/ppermute | solution.py:20
  149.3 9.1 %slice-start = ((s8[6553600]{0:T(1024)(128)(4,1)}), s8[4194304]{0:T(1024)(128)(4,1)S(1)}, s32[]{:S(2)}) async-start(s8[6553600]{0:T(1024)(128)(4,1)} %bitcast.83), calls=%async_computation | async-start | bytes 8388608
  150.0 43.1 %copy-start.3 = (f32[320,64]{1,0:T(8,128)}, f32[320,64]{1,0:T(8,128)S(1)}, u32[]{:S(2)}) copy-start(f32[320,64]{1,0:T(8,128)S(1)} %get-tuple-element.24) | copy-start | bytes 245764
  150.0 8.4 %slice-start.1 = ((s8[6553600]{0:T(1024)(128)(4,1)}), s8[2359296]{0:T(1024)(128)(4,1)S(1)}, s32[]{:S(2)}) async-start(s8[6553600]{0:T(1024)(128)(4,1)} %bitcast.83), calls=%async_computation.1 | async-start | bytes 4718592
  150.0 59.2 %collective-permute-start.11 = (bf16[2,4096,256]{2,1,0:T(8,128)(2,1)}, bf16[2,4096,256]{2,1,0:T(8,128)(2,1)}, u32[]{:S(2)}, u32[]{:S(2)}) collective-permute-start(bf16[2,4096,256]{2,1,0:T(8,128)(2,1)} %collective-permute-done.9.refs_1_), channel_id=1, source_target_pairs={{0,1},{1,0},{2,3},{3,2},{4,5},{5,4},{6,7},{7,6},{8,9},{9,8},{10,11... | collective-permute-start | bytes 12582920 | tf_op jit(solution)/shard_map/ppermute | solution.py:20
  153.9 21.2 %collective-permute-start.20 = (bf16[1,320,1280]{2,1,0:T(8,128)(2,1)S(1)}, bf16[1,320,1280]{2,1,0:T(8,128)(2,1)S(1)}, u32[]{:S(2)}, u32[]{:S(2)}) collective-permute-start(bf16[1,320,1280]{2,1,0:T(8,128)(2,1)S(1)} %dynamic-slice_convert_fusion), channel_id=1, source_target_pairs={{0,2},{1,3},{2,0},{3,1},{4,6},{5,7},{6,4},{7,5},{8,10},{9,11},{10,... | collective-permute-start | bytes 2457608 | tf_op jit(solution)/shard_map/ppermute | solution.py:20
  159.0 33.4 %collective-permute-start.8 = (bf16[1,320,1280]{2,1,0:T(8,128)(2,1)S(1)}, bf16[1,320,1280]{2,1,0:T(8,128)(2,1)S(1)}, u32[]{:S(2)}, u32[]{:S(2)}) collective-permute-start(bf16[1,320,1280]{2,1,0:T(8,128)(2,1)S(1)} %dynamic-slice_convert_fusion.1), channel_id=1, source_target_pairs={{0,2},{1,3},{2,0},{3,1},{4,6},{5,7},{6,4},{7,5},{8,10},{9,11},{10,... | collective-permute-start | bytes 2457608 | tf_op jit(solution)/shard_map/ppermute | solution.py:20
  206.2 1.4 copy-start.5
  273.9 64.6 %copy-start.4 = (bf16[320,1024]{1,0:T(8,128)(2,1)S(1)}, bf16[320,1024]{1,0:T(8,128)(2,1)}, u32[]{:S(2)}) copy-start(bf16[320,1024]{1,0:T(8,128)(2,1)} %attend.2) | copy-start | bytes 1966084
